TPU v7x, 32 devices: a whole 2x2x4 slice. The times are simulated.
32 devices in a mesh: dp: 4 (over y, x), expert: 8 (over z, core).
Axes of the slice: x: 2, y: 2, z: 4, core: 2. Of those that a mesh axis runs over, the one named last changes fastest.
Arguments:
- output_grad: bfloat16 [6144, 2048], P(('dp', 'expert')), may hold values from -3 to 3
- routes: int32 [6144, 2], P(('dp', 'expert')), may hold values from 0 to 7, all different within a row; in each aligned block of 192 rows (0 to 191, 192 to 383, ...) at most 72 rows name the same one
- combine_weights: bfloat16 [6144, 2], P(('dp', 'expert')), may hold values from 0.049804688 to 0.5
- saved_hidden: bfloat16 [18432, 768], P(('dp', 'expert')), may hold values from -0.796875 to 0.796875
- down_weight: bfloat16 [8, 768, 2048], P('expert', 'dp'), may hold values from -0.21875 to 0.21875
Outputs:
- hidden_grad: bfloat16 [18432, 768], P(('dp', 'expert'))
- weight_grad: float32 [8, 768, 2048], P('expert', 'dp')
- route_grad: float32 [6144, 2], P(('dp', 'expert'))
Inputs may be any that keep to these rules, and one draw needn't show every extreme that they name: Each token names 2 different experts; among the 192 rows of one device no expert is named by more than 72 routes.
All inputs are finite; a program needn't handle non-finite values.
Results may differ from a plain program's by a relative error of at most 0.008.
Values may be sent and summed in bfloat16 or wider, within the bound.
A program may use at most 64 MiB of HBM per device.

v0:
```python
import jax
import jax.numpy as jnp
from jax import lax
from jax.sharding import PartitionSpec as P


def route_slots(routes, experts, capacity):
    flat_ids = routes.reshape(-1)
    one_hot = (flat_ids[:, None] == jnp.arange(experts, dtype=jnp.int32)[None, :]).astype(jnp.int32)
    earlier = jnp.cumsum(one_hot, axis=0) - one_hot
    return flat_ids * capacity + jnp.sum(earlier * one_hot, axis=1)


def per_device(output_grad, routes, combine_weights, saved_hidden, down_weight):
    experts = lax.axis_size("expert")
    slot_count = saved_hidden.shape[0]
    capacity = slot_count // experts
    features = output_grad.shape[1]
    route_total = routes.shape[0] * routes.shape[1]
    target = route_slots(routes, experts, capacity)
    source = (
        jnp.full((slot_count,), route_total, jnp.int32)
        .at[target]
        .set(jnp.arange(route_total, dtype=jnp.int32))
    )
    is_live = source < route_total
    safe_index = jnp.where(is_live, source, 0)
    send_rows = jnp.where(
        is_live[:, None], output_grad[safe_index // routes.shape[1]], jnp.zeros((), jnp.bfloat16)
    )
    send_weights = jnp.where(
        is_live, combine_weights.reshape(-1)[safe_index], jnp.zeros((), jnp.bfloat16)
    )
    recv_rows, recv_weights = (
        lax.all_to_all(
            send_rows.reshape(experts, capacity, features),
            "expert",
            split_axis=0,
            concat_axis=0,
            tiled=True,
        ),
        lax.all_to_all(
            send_weights.reshape(experts, capacity),
            "expert",
            split_axis=0,
            concat_axis=0,
            tiled=True,
        ),
    )
    grad_rows = recv_rows.reshape(slot_count, features)
    slot_weights = recv_weights.reshape(slot_count).astype(jnp.float32)
    weighted = (slot_weights[:, None] * grad_rows.astype(jnp.float32)).astype(jnp.bfloat16)
    weight_shard = down_weight[0]
    contract = (((1,), (1,)), ((), ()))
    full_weight = lax.all_gather(weight_shard, "dp", axis=0, tiled=True)
    unscaled = lax.dot_general(grad_rows, full_weight, contract, preferred_element_type=jnp.float32)
    route_terms = jnp.sum(saved_hidden.astype(jnp.float32) * unscaled, axis=1)
    hidden_grad = (slot_weights[:, None] * unscaled).astype(jnp.bfloat16)
    grad_part = lax.psum_scatter(
        lax.dot_general(
            saved_hidden, weighted, (((0,), (0,)), ((), ())), preferred_element_type=jnp.float32
        ).astype(jnp.bfloat16),
        "dp",
        scatter_dimension=0,
        tiled=True,
    ).astype(jnp.float32)
    returned = lax.all_to_all(
        route_terms.reshape(experts, capacity), "expert", split_axis=0, concat_axis=0, tiled=True
    )
    route_grad = returned.reshape(-1)[target].reshape(routes.shape)
    return (hidden_grad, grad_part[None], route_grad)


def solution(mesh):
    return jax.shard_map(
        per_device,
        mesh=mesh,
        in_specs=(
            P(("dp", "expert"), None),
            P(("dp", "expert"), None),
            P(("dp", "expert"), None),
            P(("dp", "expert"), None),
            P("expert", "dp", None),
        ),
        out_specs=(P(("dp", "expert"), None), P("expert", "dp", None), P(("dp", "expert"), None)),
        check_vma=False,
    )
```

profile of v0, /device:TPU:0, one launch (start us, length us, event | category | flops | bytes accessed | tf_op | source)
XLA Modules:
  0.0 156.6 jit_solution(16098599032661356121)
XLA Ops:
  7.2 0.9 copy.16
  8.1 0.1 eq.29
  8.2 0.1 eq.25
  8.3 0.7 broadcast_multiply_fusion
  9.0 0.8 reduce-window.6
  9.9 0.2 slice_reduce_fusion
  10.3 0.1 mul.40
  10.5 2.9 %scatter_custom_fusion = s32[576]{0:T(1024)S(1)} fusion(s32[384]{0:T(512)S(1)} %fusion.11, s32[384]{0:T(512)S(1)} %iota.11, s32[]{:T(128)} %constant.12.clone.1), kind=kCustom, calls=%fused_computation.36 | custom fusion | bytes 2308 | tf_op jit(solution)/shard_map/scatter | solution.py:24
  13.5 0.8 copy.18
  14.3 0.2 reshape.91
  14.5 3.9 %gather_fusion = bf16[576]{0:T(1024)(128)(2,1)S(1)} fusion(bf16[384]{0:T(512)(128)(2,1)S(1)} %reshape.91, s32[1024]{0:T(1024)S(1)} %pad_clamp_fusion.2), kind=kCustom, calls=%fused_computation | custom fusion | bytes 4608 | tf_op jit(solution)/shard_map/gather | solution.py:32
  18.5 0.7 all_to_all.20
  19.1 6.3 %all-to-all-start = ((bf16[8,1,72]{2,1,0:T(2,128)(2,1)}), bf16[8,1,72]{2,1,0:T(2,128)(2,1)S(1)}, u32[]{:S(2)}, u32[]{:S(2)}) async-start(bf16[8,1,72]{2,1,0:T(2,128)(2,1)} %all_to_all.20), calls=%async_computation | async-start | bytes 8192 | tf_op jit(solution)/shard_map/all_to_all | solution.py:42
  25.5 0.7 all-gather.3.cloned.1.call-update
  26.3 3.4 %gather_fusion.1 = bf16[576,2048]{1,0:T(8,128)(2,1)S(1)} fusion(bf16[192,2048]{1,0:T(8,128)(2,1)S(1)} %copy-done, s32[1024]{0:T(1024)S(1)} %pad_clamp_fusion.1), kind=kCustom, calls=%fused_computation.1 | custom fusion | bytes 4720896 | tf_op jit(solution)/shard_map/gather | solution.py:29
  29.7 1.7 %broadcast_select_fusion = bf16[8,72,2048]{2,1,0:T(8,128)(2,1)} fusion(bf16[8,72,2048]{2,1,0:T(8,128)(2,1)S(1)} %bitcast.24, pred[8,72]{1,0:T(8,128)(4,1)S(1)} %broadcast_in_dim.43), kind=kLoop, calls=%fused_computation.10 | loop fusion | flops 1179648 | bytes 4719168 | tf_op jit(solution)/shard_map/jit(_where)/select_n | solution.py:28
  31.4 5.1 %all-to-all-start.1 = ((bf16[8,72,2048]{2,1,0:T(8,128)(2,1)}), bf16[8,72,2048]{2,1,0:T(8,128)(2,1)S(1)}, u32[]{:S(2)}, u32[]{:S(2)}) async-start(bf16[8,72,2048]{2,1,0:T(8,128)(2,1)} %broadcast_select_fusion), calls=%async_computation.1 | async-start | bytes 4718592 | tf_op jit(solution)/shard_map/all_to_all | solution.py:35
  36.6 54.5 %all-to-all-done.1 = bf16[8,72,2048]{2,1,0:T(8,128)(2,1)S(1)} async-done(((bf16[8,72,2048]{2,1,0:T(8,128)(2,1)}), bf16[8,72,2048]{2,1,0:T(8,128)(2,1)S(1)}, u32[]{:S(2)}, u32[]{:S(2)}) %all-to-all-start.1) | async-done | bytes 2359328 | tf_op jit(solution)/shard_map/all_to_all | solution.py:35
  91.2 5.5 %fusion.2 = bf16[768,2048]{0,1:T(8,128)(2,1)} fusion(bf16[576,768]{1,0:T(8,128)(2,1)} %param.8, bf16[576,2048]{1,0:T(8,128)(2,1)S(1)} %bitcast.25, f32[576]{0:T(1024)S(1)} %reshape.95), kind=kOutput, calls=%fused_computation.8 | convolution fusion | flops 1817051136 | bytes 6392064 | tf_op jit(solution)/shard_map/dot_general | solution.py:60
  96.7 4.7 %copy.22 = bf16[768,2048]{1,0:T(8,128)(2,1)} copy(bf16[768,2048]{0,1:T(8,128)(2,1)} %fusion.2) | data formatting | bytes 6291456
  101.5 5.1 %multiply_reduce_fusion = (f32[576]{0:T(1024)S(1)}, bf16[576,768]{1,0:T(8,128)(2,1)}) fusion(bf16[576,768]{1,0:T(8,128)(2,1)} %param.8, f32[576]{0:T(1024)S(1)} %reshape.95, bf16[576,2048]{1,0:T(8,128)(2,1)S(1)} %bitcast.26, bf16[1,768,2048]{2,1,0:T(8,128)(2,1)} %all-gather.3.cloned.1.call-done), kind=kOutput, calls=%fused_computation.11 | convolution fusion | flops 1814150656 | bytes 7279104 | tf_op jit(solution)/shard_map/dot_general | solution.py:56
  106.5 0.7 all_to_all.18
  107.2 3.3 %all-to-all-start.2 = ((f32[8,1,72]{2,1,0:T(1,128)}), f32[8,1,72]{2,1,0:T(1,128)S(1)}, u32[]{:S(2)}, u32[]{:S(2)}) async-start(f32[8,1,72]{2,1,0:T(1,128)} %all_to_all.18), calls=%async_computation.2 | async-start | bytes 8192 | tf_op jit(solution)/shard_map/all_to_all | solution.py:67
  110.6 5.4 %all-to-all-done.2 = f32[8,1,72]{2,1,0:T(1,128)S(1)} async-done(((f32[8,1,72]{2,1,0:T(1,128)}), f32[8,1,72]{2,1,0:T(1,128)S(1)}, u32[]{:S(2)}, u32[]{:S(2)}) %all-to-all-start.2) | async-done | bytes 2336 | tf_op jit(solution)/shard_map/all_to_all | solution.py:67
  116.0 0.5 broadcast.88
  116.5 0.7 reduce.11
  117.2 1.9 %gather_fusion.2 = f32[384]{0:T(512)S(1)} fusion(f32[576]{0:T(1024)S(1)} %reshape.93, s32[1024]{0:T(1024)S(1)} %pad_clamp_fusion), kind=kCustom, calls=%fused_computation.2 | custom fusion | bytes 4608 | tf_op jit(solution)/shard_map/gather | solution.py:70
  119.2 0.7 copy.21
  119.9 24.6 %reduce-scatter.4.cloned.1.call-done = bf16[192,2048]{1,0:T(8,128)(2,1)} async-done(((bf16[768,2048]{1,0:T(8,128)(2,1)}), bf16[192,2048]{1,0:T(8,128)(2,1)}) %reduce-scatter.4.cloned.1.call-update) | async-done | bytes 786448
  144.5 2.2 %copy.23 = bf16[192,2048]{0,1:T(8,128)(2,1)} copy(bf16[192,2048]{1,0:T(8,128)(2,1)} %reduce-scatter.4.cloned.1.call-done) | data formatting | bytes 1572864
  146.7 1.4 bitcast_convert_fusion
  148.1 1.7 %copy.20 = f32[1,192,2048]{2,1,0:T(8,128)} copy(f32[1,192,2048]{1,2,0:T(8,128)S(1)} %bitcast_convert_fusion) | data formatting | bytes 3145728
  (24 shorter events, 0.8 us)
Async XLA Ops:
  7.2 19.1 %copy-start = (bf16[192,2048]{1,0:T(8,128)(2,1)S(1)}, bf16[192,2048]{1,0:T(8,128)(2,1)}, u32[]{:S(2)}) copy-start(bf16[192,2048]{1,0:T(8,128)(2,1)} %param.5) | copy-start | bytes 2359300
  19.1 12.3 %all-to-all-start = ((bf16[8,1,72]{2,1,0:T(2,128)(2,1)}), bf16[8,1,72]{2,1,0:T(2,128)(2,1)S(1)}, u32[]{:S(2)}, u32[]{:S(2)}) async-start(bf16[8,1,72]{2,1,0:T(2,128)(2,1)} %all_to_all.20), calls=%async_computation | async-start | bytes 8192 | tf_op jit(solution)/shard_map/all_to_all | solution.py:42
  25.5 76.0 %all-gather.3.cloned.1.call-start = ((), (), s32[]{:S(2)}) async-start(), calls=%async_computation.4 | async-start | bytes 3932160 | tf_op jit(solution)/shard_map/all_gather | solution.py:55
  31.4 59.8 %all-to-all-start.1 = ((bf16[8,72,2048]{2,1,0:T(8,128)(2,1)}), bf16[8,72,2048]{2,1,0:T(8,128)(2,1)S(1)}, u32[]{:S(2)}, u32[]{:S(2)}) async-start(bf16[8,72,2048]{2,1,0:T(8,128)(2,1)} %broadcast_select_fusion), calls=%async_computation.1 | async-start | bytes 4718592 | tf_op jit(solution)/shard_map/all_to_all | solution.py:35
  36.5 108.0 %reduce-scatter.4.cloned.1.call-start = ((), (), s32[]{:S(2)}) async-start(), calls=%async_computation.5 | async-start | bytes 3932160
  107.2 8.7 %all-to-all-start.2 = ((f32[8,1,72]{2,1,0:T(1,128)}), f32[8,1,72]{2,1,0:T(1,128)S(1)}, u32[]{:S(2)}, u32[]{:S(2)}) async-start(f32[8,1,72]{2,1,0:T(1,128)} %all_to_all.18), calls=%async_computation.2 | async-start | bytes 8192 | tf_op jit(solution)/shard_map/all_to_all | solution.py:67
Sparse Core Ops, SparseCore 0:
  28.1 45.4 all-gather.2
  101.6 42.8 reduce-scatter.3
where the time goes:
time: 157 us
  waiting for transfers between devices  85.2 us (54%)
  local copies, waits for them, and re-layouts  26.3 us (17%)
  starting transfers between devices  14.8 us (9%)
  between operations  14.2 us (9%)
  matrix products  10.6 us (7%)
  other arithmetic  5.47 us (3%)
    all_to_all x1, waiting for transfers between devices, per_device(): lax.all_to_all(send_rows.reshape(experts, capacity, features), 'expert',...  54.5 us
    unnamed x3, waiting for transfers between devices  25.3 us
    unnamed x8, local copies, waits for them, and re-layouts  11 us
    all_to_all x1, starting transfers between devices, per_device(): lax.all_to_all(send_weights.reshape(experts, capacity), 'expert', split_a...  6.33 us
    dot_general x1, matrix products, per_device(): lax.dot_general(saved_hidden, weighted, (((0,), (0,)), ((), ())), preferr...  5.53 us
    all_to_all x1, waiting for transfers between devices, per_device(): lax.all_to_all(route_terms.reshape(experts, capacity), 'expert', split_ax...  5.4 us
    all_to_all x1, starting transfers between devices, per_device(): lax.all_to_all(send_rows.reshape(experts, capacity, features), 'expert',...  5.09 us
    dot_general x1, matrix products, per_device(): lax.dot_general(grad_rows, full_weight, contract, preferred_element_type=...  5.08 us
  transfers between devices with their start and end apart: 5, of which 3 were waited for; matrix products, arithmetic and copies ran while one was open for 16% of the time, Pallas kernels for 0%

commit v1 on v0

--- a/solution.py
+++ b/solution.py
@@ -2,6 +2,22 @@
 import jax.numpy as jnp
 from jax import lax
 from jax.sharding import PartitionSpec as P
+
+
+def exchange_in_pairs(array, axis, split, join):
+    ways, here = (lax.axis_size(axis), lax.axis_index(axis))
+    width = array.shape[split] // ways
+    shape = list(array.shape)
+    shape[split] = width
+    height = shape[join]
+    shape[join] = height * ways
+    full = jnp.zeros(shape, array.dtype)
+    for mask in range(ways):
+        part = lax.dynamic_slice_in_dim(array, (here ^ mask) * width, width, axis=split)
+        if mask:
+            part = lax.ppermute(part, axis, [(d, d ^ mask) for d in range(ways)])
+        full = lax.dynamic_update_slice_in_dim(full, part, (here ^ mask) * height, axis=join)
+    return full
 
 
 def route_slots(routes, experts, capacity):
@@ -39,13 +55,7 @@
             concat_axis=0,
             tiled=True,
         ),
-        lax.all_to_all(
-            send_weights.reshape(experts, capacity),
-            "expert",
-            split_axis=0,
-            concat_axis=0,
-            tiled=True,
-        ),
+        exchange_in_pairs(send_weights.reshape(experts, capacity), "expert", 0, 0),
     )
     grad_rows = recv_rows.reshape(slot_count, features)
     slot_weights = recv_weights.reshape(slot_count).astype(jnp.float32)

time: 157 us -> 147 us (0.936)
  waiting for transfers between devices: 85.2 us -> 69.7 us
  starting transfers between devices: 14.8 us -> 21 us
    all_to_all x1, waiting for transfers between devices: 54.5 us -> 0.01 us  [per_device(): lax.all_to_all(send_rows.reshape(experts, capacity, features), 'expert',...]
    ppermute x0 -> x7, waiting for transfers between devices: none -> 39.1 us  [exchange_in_pairs(): part = lax.ppermute(part, axis, [(d, d ^ mask) for d in range(ways)])]
    ppermute x0 -> x7, starting transfers between devices: none -> 11.1 us  [exchange_in_pairs(): part = lax.ppermute(part, axis, [(d, d ^ mask) for d in range(ways)])]
    all_to_all x1 -> x0, starting transfers between devices: 6.33 us -> none  [per_device(): lax.all_to_all(send_weights.reshape(experts, capacity), 'expert', split_a...]
    unnamed x8 -> x10, local copies, waits for them, and re-layouts: 11 us -> 10.2 us
  transfers between devices with their start and end apart: 5 -> 11, of which waited for: 3 -> 4; matrix products, arithmetic and copies ran while one was open for 16% -> 24% of each run, Pallas kernels for 0% -> 0%
where the time goes in v1:
time: 147 us; the launch traced here: 146 us
  waiting for transfers between devices  69.7 us (47%)
  local copies, waits for them, and re-layouts  25.2 us (17%)
  starting transfers between devices  21 us (14%)
  between operations  14.3 us (10%)
  matrix products  10.6 us (7%)
  other arithmetic  5.48 us (4%)
    ppermute x7, waiting for transfers between devices, exchange_in_pairs(): part = lax.ppermute(part, axis, [(d, d ^ mask) for d in range(ways)])  39.1 us
    unnamed x3, waiting for transfers between devices  25.3 us
    ppermute x7, starting transfers between devices, exchange_in_pairs(): part = lax.ppermute(part, axis, [(d, d ^ mask) for d in range(ways)])  11.1 us
    unnamed x10, local copies, waits for them, and re-layouts  10.2 us
    all_to_all x1, starting transfers between devices, per_device(): lax.all_to_all(send_rows.reshape(experts, capacity, features), 'expert',...  6.46 us
    dot_general x1, matrix products, per_device(): lax.dot_general(saved_hidden, weighted, (((0,), (0,)), ((), ())), preferr...  5.53 us
    all_to_all x1, waiting for transfers between devices, per_device(): lax.all_to_all(route_terms.reshape(experts, capacity), 'expert', split_ax...  5.4 us
    dot_general x1, matrix products, per_device(): lax.dot_general(grad_rows, full_weight, contract, preferred_element_type=...  5.08 us
  transfers between devices with their start and end apart: 11, of which 4 were waited for; matrix products, arithmetic and copies ran while one was open for 24% of the time, Pallas kernels for 0%

profile of v1, /device:TPU:0, one launch (start us, length us, event | category | flops | bytes accessed | tf_op | source)
XLA Modules:
  0.0 146.3 jit_solution(6730096498077929742)
XLA Ops:
  7.2 0.7 all-gather.3.cloned.1.call-update
  7.9 0.7 broadcast_multiply_fusion
  8.6 0.8 copy.16
  10.0 0.9 reduce-window.6
  10.8 0.2 slice_reduce_fusion
  11.2 2.9 %scatter_custom_fusion = s32[576]{0:T(1024)S(1)} fusion(s32[384]{0:T(512)S(1)} %fusion.11, s32[384]{0:T(512)S(1)} %iota.11, s32[]{:T(128)} %constant.18.clone.1), kind=kCustom, calls=%fused_computation.43 | custom fusion | bytes 2308 | tf_op jit(solution)/shard_map/scatter | solution.py:40
  14.3 3.4 %gather_fusion.1 = bf16[576,2048]{1,0:T(8,128)(2,1)S(1)} fusion(bf16[192,2048]{1,0:T(8,128)(2,1)S(1)} %copy-done, s32[1024]{0:T(1024)S(1)} %pad_clamp_fusion.1), kind=kCustom, calls=%fused_computation.1 | custom fusion | bytes 4720896 | tf_op jit(solution)/shard_map/gather | solution.py:45
  17.7 1.7 %broadcast_select_fusion = bf16[8,72,2048]{2,1,0:T(8,128)(2,1)} fusion(bf16[8,72,2048]{2,1,0:T(8,128)(2,1)S(1)} %bitcast.24, pred[8,72]{1,0:T(8,128)(4,1)S(1)} %broadcast_in_dim.47), kind=kLoop, calls=%fused_computation.10 | loop fusion | flops 1179648 | bytes 4719168 | tf_op jit(solution)/shard_map/jit(_where)/select_n | solution.py:44
  19.4 6.5 %all-to-all-start = ((bf16[8,72,2048]{2,1,0:T(8,128)(2,1)}), bf16[8,72,2048]{2,1,0:T(8,128)(2,1)S(1)}, u32[]{:S(2)}, u32[]{:S(2)}) async-start(bf16[8,72,2048]{2,1,0:T(8,128)(2,1)} %broadcast_select_fusion), calls=%async_computation | async-start | bytes 4718592 | tf_op jit(solution)/shard_map/all_to_all | solution.py:51
  26.1 0.2 reshape.89
  26.3 3.9 %gather_fusion = bf16[576]{0:T(1024)(128)(2,1)S(1)} fusion(bf16[384]{0:T(512)(128)(2,1)S(1)} %reshape.89, s32[1024]{0:T(1024)S(1)} %pad_clamp_fusion.2), kind=kCustom, calls=%fused_computation | custom fusion | bytes 4608 | tf_op jit(solution)/shard_map/gather | solution.py:48
  30.3 0.5 collective-permute-start
  30.8 1.7 %collective-permute-start.1 = (bf16[1,72]{1,0:T(2,128)(2,1)S(1)}, bf16[1,72]{1,0:T(2,128)(2,1)S(1)}, u32[]{:S(2)}, u32[]{:S(2)}) collective-permute-start(bf16[1,72]{1,0:T(2,128)(2,1)S(1)} %get-tuple-element.21), channel_id=1, source_target_pairs={{0,2},{1,3},{2,0},{3,1},{4,6},{5,7},{6,4},{7,5},{8,10},{9,11},{10,... | collective-permute-start | bytes 440 | tf_op jit(solution)/shard_map/ppermute | solution.py:18
  32.5 2.6 %collective-permute-start.3 = (bf16[1,72]{1,0:T(2,128)(2,1)S(1)}, bf16[1,72]{1,0:T(2,128)(2,1)S(1)}, u32[]{:S(2)}, u32[]{:S(2)}) collective-permute-start(bf16[1,72]{1,0:T(2,128)(2,1)S(1)} %get-tuple-element.19), channel_id=1, source_target_pairs={{0,4},{1,5},{2,6},{3,7},{4,0},{5,1},{6,2},{7,3},{8,12},{9,13},{10,... | collective-permute-start | bytes 440 | tf_op jit(solution)/shard_map/ppermute | solution.py:18
  35.3 3.5 %collective-permute-start.5 = (bf16[1,72]{1,0:T(2,128)(2,1)S(1)}, bf16[1,72]{1,0:T(2,128)(2,1)S(1)}, u32[]{:S(2)}, u32[]{:S(2)}) collective-permute-start(bf16[1,72]{1,0:T(2,128)(2,1)S(1)} %get-tuple-element.17), channel_id=1, source_target_pairs={{0,6},{1,7},{2,4},{3,5},{4,2},{5,3},{6,0},{7,1},{8,14},{9,15},{10,... | collective-permute-start | bytes 440 | tf_op jit(solution)/shard_map/ppermute | solution.py:18
  38.8 26.2 %collective-permute-done.1 = bf16[1,72]{1,0:T(2,128)(2,1)S(1)} collective-permute-done((bf16[1,72]{1,0:T(2,128)(2,1)S(1)}, bf16[1,72]{1,0:T(2,128)(2,1)S(1)}, u32[]{:S(2)}, u32[]{:S(2)}) %collective-permute-start.1) | collective-permute-done | bytes 176 | tf_op jit(solution)/shard_map/ppermute | solution.py:18
  65.0 2.7 %collective-permute-start.6 = (bf16[1,72]{1,0:T(2,128)(2,1)S(1)}, bf16[1,72]{1,0:T(2,128)(2,1)S(1)}, u32[]{:S(2)}, u32[]{:S(2)}) collective-permute-start(bf16[1,72]{1,0:T(2,128)(2,1)S(1)} %get-tuple-element.16), channel_id=1, source_target_pairs={{0,7},{1,6},{2,5},{3,4},{4,3},{5,2},{6,1},{7,0},{8,15},{9,14},{10,... | collective-permute-start | bytes 440 | tf_op jit(solution)/shard_map/ppermute | solution.py:18
  67.8 12.8 %collective-permute-done.3 = bf16[1,72]{1,0:T(2,128)(2,1)S(1)} collective-permute-done((bf16[1,72]{1,0:T(2,128)(2,1)S(1)}, bf16[1,72]{1,0:T(2,128)(2,1)S(1)}, u32[]{:S(2)}, u32[]{:S(2)}) %collective-permute-start.3) | collective-permute-done | bytes 176 | tf_op jit(solution)/shard_map/ppermute | solution.py:18
  80.9 5.5 %fusion.2 = bf16[768,2048]{0,1:T(8,128)(2,1)} fusion(bf16[576,768]{1,0:T(8,128)(2,1)} %param.8, bf16[576,2048]{1,0:T(8,128)(2,1)S(1)} %bitcast.25, f32[576]{0:T(1024)S(1)} %reshape.94), kind=kOutput, calls=%fused_computation.8 | convolution fusion | flops 1817051136 | bytes 6392064 | tf_op jit(solution)/shard_map/dot_general | solution.py:70
  86.4 4.7 %copy.21 = bf16[768,2048]{1,0:T(8,128)(2,1)} copy(bf16[768,2048]{0,1:T(8,128)(2,1)} %fusion.2) | data formatting | bytes 6291456
  91.2 5.1 %multiply_reduce_fusion = (f32[576]{0:T(1024)S(1)}, bf16[576,768]{1,0:T(8,128)(2,1)}) fusion(bf16[576,768]{1,0:T(8,128)(2,1)} %param.8, f32[576]{0:T(1024)S(1)} %reshape.94, bf16[576,2048]{1,0:T(8,128)(2,1)S(1)} %bitcast.26, bf16[1,768,2048]{2,1,0:T(8,128)(2,1)} %all-gather.3.cloned.1.call-done), kind=kOutput, calls=%fused_computation.11 | convolution fusion | flops 1814150656 | bytes 7279104 | tf_op jit(solution)/shard_map/dot_general | solution.py:66
  96.3 0.7 all_to_all.10
  96.9 3.3 %all-to-all-start.1 = ((f32[8,1,72]{2,1,0:T(1,128)}), f32[8,1,72]{2,1,0:T(1,128)S(1)}, u32[]{:S(2)}, u32[]{:S(2)}) async-start(f32[8,1,72]{2,1,0:T(1,128)} %all_to_all.10), calls=%async_computation.1 | async-start | bytes 8192 | tf_op jit(solution)/shard_map/all_to_all | solution.py:77
  100.3 5.4 %all-to-all-done.1 = f32[8,1,72]{2,1,0:T(1,128)S(1)} async-done(((f32[8,1,72]{2,1,0:T(1,128)}), f32[8,1,72]{2,1,0:T(1,128)S(1)}, u32[]{:S(2)}, u32[]{:S(2)}) %all-to-all-start.1) | async-done | bytes 2336 | tf_op jit(solution)/shard_map/all_to_all | solution.py:77
  105.7 0.5 broadcast.89
  106.2 0.7 reduce.7
  106.9 1.9 %gather_fusion.2 = f32[384]{0:T(512)S(1)} fusion(f32[576]{0:T(1024)S(1)} %reshape.92, s32[1024]{0:T(1024)S(1)} %pad_clamp_fusion), kind=kCustom, calls=%fused_computation.2 | custom fusion | bytes 4608 | tf_op jit(solution)/shard_map/gather | solution.py:80
  109.0 0.7 copy.20
  109.6 24.6 %reduce-scatter.4.cloned.1.call-done = bf16[192,2048]{1,0:T(8,128)(2,1)} async-done(((bf16[768,2048]{1,0:T(8,128)(2,1)}), bf16[192,2048]{1,0:T(8,128)(2,1)}) %reduce-scatter.4.cloned.1.call-update) | async-done | bytes 786448
  134.2 2.2 %copy.22 = bf16[192,2048]{0,1:T(8,128)(2,1)} copy(bf16[192,2048]{1,0:T(8,128)(2,1)} %reduce-scatter.4.cloned.1.call-done) | data formatting | bytes 1572864
  136.4 1.4 bitcast_convert_fusion
  137.8 1.7 %copy.19 = f32[1,192,2048]{2,1,0:T(8,128)} copy(f32[1,192,2048]{1,2,0:T(8,128)S(1)} %bitcast_convert_fusion) | data formatting | bytes 3145728
  (47 shorter events, 1.9 us)
Async XLA Ops:
  7.2 7.1 %copy-start = (bf16[192,2048]{1,0:T(8,128)(2,1)S(1)}, bf16[192,2048]{1,0:T(8,128)(2,1)}, u32[]{:S(2)}) copy-start(bf16[192,2048]{1,0:T(8,128)(2,1)} %param.5) | copy-start | bytes 2359300
  7.2 84.0 %all-gather.3.cloned.1.call-start = ((), (), s32[]{:S(2)}) async-start(), calls=%async_computation.3 | async-start | bytes 3932160 | tf_op jit(solution)/shard_map/all_gather | solution.py:65
  19.4 6.5 %copy-start.1 = (bf16[192,2]{0,1:T(2,128)(2,1)S(1)}, bf16[192,2]{0,1:T(2,128)(2,1)}, u32[]{:S(2)}) copy-start(bf16[192,2]{0,1:T(2,128)(2,1)} %param.7) | copy-start | bytes 2308
  19.4 61.5 %all-to-all-start = ((bf16[8,72,2048]{2,1,0:T(8,128)(2,1)}), bf16[8,72,2048]{2,1,0:T(8,128)(2,1)S(1)}, u32[]{:S(2)}, u32[]{:S(2)}) async-start(bf16[8,72,2048]{2,1,0:T(8,128)(2,1)} %broadcast_select_fusion), calls=%async_computation | async-start | bytes 4718592 | tf_op jit(solution)/shard_map/all_to_all | solution.py:51
  25.8 108.3 %reduce-scatter.4.cloned.1.call-start = ((), (), s32[]{:S(2)}) async-start(), calls=%async_computation.4 | async-start | bytes 3932160
  30.3 4.9 %collective-permute-start = (bf16[1,72]{1,0:T(2,128)(2,1)S(1)}, bf16[1,72]{1,0:T(2,128)(2,1)S(1)}, u32[]{:S(2)}, u32[]{:S(2)}) collective-permute-start(bf16[1,72]{1,0:T(2,128)(2,1)S(1)} %get-tuple-element.22), channel_id=1, source_target_pairs={{0,1},{1,0},{2,3},{3,2},{4,5},{5,4},{6,7},{7,6},{8,9},{9,8},{10,11... | collective-permute-start | bytes 440 | tf_op jit(solution)/shard_map/ppermute | solution.py:18
  30.8 34.2 %collective-permute-start.1 = (bf16[1,72]{1,0:T(2,128)(2,1)S(1)}, bf16[1,72]{1,0:T(2,128)(2,1)S(1)}, u32[]{:S(2)}, u32[]{:S(2)}) collective-permute-start(bf16[1,72]{1,0:T(2,128)(2,1)S(1)} %get-tuple-element.21), channel_id=1, source_target_pairs={{0,2},{1,3},{2,0},{3,1},{4,6},{5,7},{6,4},{7,5},{8,10},{9,11},{10,... | collective-permute-start | bytes 440 | tf_op jit(solution)/shard_map/ppermute | solution.py:18
  32.5 35.3 %collective-permute-start.2 = (bf16[1,72]{1,0:T(2,128)(2,1)S(1)}, bf16[1,72]{1,0:T(2,128)(2,1)S(1)}, u32[]{:S(2)}, u32[]{:S(2)}) collective-permute-start(bf16[1,72]{1,0:T(2,128)(2,1)S(1)} %get-tuple-element.20), channel_id=1, source_target_pairs={{0,3},{1,2},{2,1},{3,0},{4,7},{5,6},{6,5},{7,4},{8,11},{9,10},{10,... | collective-permute-start | bytes 440 | tf_op jit(solution)/shard_map/ppermute | solution.py:18
  32.5 48.1 %collective-permute-start.3 = (bf16[1,72]{1,0:T(2,128)(2,1)S(1)}, bf16[1,72]{1,0:T(2,128)(2,1)S(1)}, u32[]{:S(2)}, u32[]{:S(2)}) collective-permute-start(bf16[1,72]{1,0:T(2,128)(2,1)S(1)} %get-tuple-element.19), channel_id=1, source_target_pairs={{0,4},{1,5},{2,6},{3,7},{4,0},{5,1},{6,2},{7,3},{8,12},{9,13},{10,... | collective-permute-start | bytes 440 | tf_op jit(solution)/shard_map/ppermute | solution.py:18
  35.1 45.6 %collective-permute-start.4 = (bf16[1,72]{1,0:T(2,128)(2,1)S(1)}, bf16[1,72]{1,0:T(2,128)(2,1)S(1)}, u32[]{:S(2)}, u32[]{:S(2)}) collective-permute-start(bf16[1,72]{1,0:T(2,128)(2,1)S(1)} %get-tuple-element.18), channel_id=1, source_target_pairs={{0,5},{1,4},{2,7},{3,6},{4,1},{5,0},{6,3},{7,2},{8,13},{9,12},{10,... | collective-permute-start | bytes 440 | tf_op jit(solution)/shard_map/ppermute | solution.py:18
  35.3 45.5 %collective-permute-start.5 = (bf16[1,72]{1,0:T(2,128)(2,1)S(1)}, bf16[1,72]{1,0:T(2,128)(2,1)S(1)}, u32[]{:S(2)}, u32[]{:S(2)}) collective-permute-start(bf16[1,72]{1,0:T(2,128)(2,1)S(1)} %get-tuple-element.17), channel_id=1, source_target_pairs={{0,6},{1,7},{2,4},{3,5},{4,2},{5,3},{6,0},{7,1},{8,14},{9,15},{10,... | collective-permute-start | bytes 440 | tf_op jit(solution)/shard_map/ppermute | solution.py:18
  65.0 15.7 %collective-permute-start.6 = (bf16[1,72]{1,0:T(2,128)(2,1)S(1)}, bf16[1,72]{1,0:T(2,128)(2,1)S(1)}, u32[]{:S(2)}, u32[]{:S(2)}) collective-permute-start(bf16[1,72]{1,0:T(2,128)(2,1)S(1)} %get-tuple-element.16), channel_id=1, source_target_pairs={{0,7},{1,6},{2,5},{3,4},{4,3},{5,2},{6,1},{7,0},{8,15},{9,14},{10,... | collective-permute-start | bytes 440 | tf_op jit(solution)/shard_map/ppermute | solution.py:18
  96.9 8.7 %all-to-all-start.1 = ((f32[8,1,72]{2,1,0:T(1,128)}), f32[8,1,72]{2,1,0:T(1,128)S(1)}, u32[]{:S(2)}, u32[]{:S(2)}) async-start(f32[8,1,72]{2,1,0:T(1,128)} %all_to_all.10), calls=%async_computation.1 | async-start | bytes 8192 | tf_op jit(solution)/shard_map/all_to_all | solution.py:77
Sparse Core Ops, SparseCore 0:
  9.9 46.6 all-gather.2
  91.3 42.8 reduce-scatter.3
